TPU v7x, 128 devices: a whole 4x4x4 slice. The times are simulated.
128 devices in a mesh: row: 16 (over z, y_hi, core), col: 8 (over x, y_lo).
Axes of the slice: x: 4, y: 4 (y_hi: 2, y_lo: 2; y = y_hi * 2 + y_lo), z: 4, core: 2. Of those that a mesh axis runs over, the one named last changes fastest.
Arguments:
- roll_hidden: bfloat16 [5376, 4096], P(('row', 'col')), may hold values from -6 to 6
- roll_cotangent: bfloat16 [5376, 4096], P(('row', 'col')), may hold values from -6 to 6
- lengths: int32 [128], P(('row', 'col')), may hold values from 1 to 42, as said below
- owners: int32 [128], P(('row', 'col')), may hold values from 0 to 15, as said below
- prompts: int32 [128], P(('row', 'col')), may hold values from 0 to 15
- rewards: float32 [128], P(('row', 'col')), may hold values from -5 to 5
- gate_weight: bfloat16 [4096, 14784], P('col', 'row'), may hold values from -0.09375 to 0.09375
- up_weight: bfloat16 [4096, 14784], P('col', 'row'), may hold values from -0.09375 to 0.09375
- down_weight: bfloat16 [14784, 4096], P('row', 'col'), may hold values from -0.046875 to 0.046875
Outputs:
- grad_input: bfloat16 [2048, 4096], P('row', 'col')
- grad_gate: bfloat16 [4096, 14784], P('col', 'row')
- grad_up: bfloat16 [4096, 14784], P('col', 'row')
- grad_down: bfloat16 [14784, 4096], P('row', 'col')
Inputs may be any that keep to these rules, and one draw needn't show every extreme that they name: `owners`: each owner value names exactly 8 rows; the lengths of one owner's rows sum to at most 128, and to exactly 128 for some owner in every draw. `lengths`: some row has length 42 in every draw.
All inputs are finite; a program needn't handle non-finite values.
Results may differ from a plain program's by a relative error of at most 0.025.
Values may be sent and summed in bfloat16 or wider, within the bound.
No kernel may reach another device: no remote copies, remote signals or barrier semaphores. Data moves between devices by JAX's collectives and lax.ppermute only.
A program may use at most 128 MiB of HBM per device.

v0:
```python
import jax
import jax.numpy as jnp
from jax import lax
from jax.sharding import PartitionSpec as P

CAPR = 128
spread_floor = 0.7


def in_one_piece(arrays, axis, split_dim, concat_dim, along):
    ends, at = ([], 0)
    for a in arrays[:-1]:
        at += a.shape[along]
        ends.append(at)
    both = jnp.concatenate(arrays, axis=along)
    return tuple(
        jnp.split(
            lax.all_to_all(both, axis, split_axis=split_dim, concat_axis=concat_dim, tiled=True),
            ends,
            axis=along,
        )
    )


def sent_together(arrays, axis, dim, along):
    widths = [a.shape[along] for a in arrays]
    both = jnp.concatenate(arrays, axis=along)
    result = lax.all_gather(both, axis, axis=dim, tiled=True)
    return tuple(jnp.split(result, [sum(widths[:k]) for k in range(1, len(widths))], axis=along))


def cut_along(array, dim, size):
    lengths = array.shape
    tiles = array.reshape(*lengths[:dim], size, lengths[dim] // size, *lengths[dim + 1 :])
    return jnp.moveaxis(tiles, dim, 0)


def sent_and_summed(array, axis, dim):
    size = lax.axis_size(axis)
    tiles = lax.all_to_all(cut_along(array, dim, size), axis, 0, 0, tiled=True)
    return jnp.sum(tiles.astype(jnp.float32), axis=0)


def row_weights(lengths, prompts, rewards, count_prompts):
    onehot = (prompts[:, None] == jnp.arange(count_prompts, dtype=jnp.int32)[None, :]).astype(
        jnp.float32
    )
    counts = jnp.maximum(jnp.sum(onehot, 0), 1.0)
    means = jnp.sum(onehot * rewards[:, None], 0) / counts
    centred = rewards - jnp.sum(onehot * means[None, :], 1)
    spreads = jnp.sqrt(jnp.sum(onehot * (centred * centred)[:, None], 0) / counts)
    divisor = jnp.maximum(jnp.sum(onehot * spreads[None, :], 1), spread_floor)
    return centred / divisor / lengths.astype(jnp.float32)


def row_offsets(lengths, owners):
    count = lengths.shape[0]
    places = jnp.arange(count, dtype=jnp.int32)
    earlier = (owners[None, :] == owners[:, None]) & (places[None, :] < places[:, None])
    return jnp.sum(jnp.where(earlier, lengths[None, :], 0), 1)


def source_index(lengths, owners, offsets, slot_count, capacity, total):
    count = lengths.shape[0]
    slots = jnp.arange(slot_count, dtype=jnp.int32)
    live = slots[None, :] < lengths[:, None]
    target = jnp.where(live, owners[:, None] * capacity + offsets[:, None] + slots[None, :], total)
    flat_source = slots[None, :] * count + jnp.arange(count, dtype=jnp.int32)[:, None]
    empty = jnp.full((total,), slot_count * count, jnp.int32)
    return empty.at[target.reshape(-1)].set(flat_source.reshape(-1), mode="drop")


def per_device(
    roll_hidden,
    roll_cotangent,
    lengths,
    owners,
    prompts,
    rewards,
    gate_weight,
    up_weight,
    down_weight,
):
    row_count = lax.axis_size("row")
    col_count = lax.axis_size("col")
    total_tokens = row_count * CAPR
    count_prompts = row_count * col_count // 8
    slot_count = roll_hidden.shape[0]
    width = roll_hidden.shape[1] // col_count
    local = jnp.stack(
        [
            lengths.astype(jnp.float32),
            owners.astype(jnp.float32),
            prompts.astype(jnp.float32),
            rewards,
        ],
        axis=1,
    )
    table = lax.all_gather(local, ("row", "col"), axis=0, tiled=True)
    all_lengths = table[:, 0].astype(jnp.int32)
    all_owners = table[:, 1].astype(jnp.int32)
    all_prompts = table[:, 2].astype(jnp.int32)
    weights = row_weights(all_lengths, all_prompts, table[:, 3], count_prompts)
    offsets = row_offsets(all_lengths, all_owners)
    mine = lax.dynamic_slice_in_dim(weights, lax.axis_index(("row", "col")), 1, 0)
    live = (jnp.arange(slot_count, dtype=jnp.int32) < lengths[0])[:, None]
    upstream = jnp.where(live, roll_cotangent.astype(jnp.float32) * mine[0], 0.0).astype(
        jnp.bfloat16
    )
    hidden_blocks = roll_hidden.reshape(slot_count, col_count, width)
    upstream_blocks = upstream.reshape(slot_count, col_count, width)
    hidden_cols, upstream_cols = in_one_piece((hidden_blocks, upstream_blocks), "col", 1, 1, 0)
    hidden_all, upstream_all = sent_together((hidden_cols, upstream_cols), "row", 1, 0)
    sources = source_index(all_lengths, all_owners, offsets, slot_count, CAPR, total_tokens)
    packed = jnp.take(hidden_all.reshape(-1, width), sources, axis=0, mode="fill", fill_value=0)
    packed_grad = jnp.take(
        upstream_all.reshape(-1, width), sources, axis=0, mode="fill", fill_value=0
    )
    gate_term = jnp.dot(packed, gate_weight, preferred_element_type=jnp.float32)
    up_term = jnp.dot(packed, up_weight, preferred_element_type=jnp.float32)
    gate, upval = (
        lax.psum(gate_term.astype(jnp.bfloat16), "col").astype(jnp.float32),
        lax.psum(up_term.astype(jnp.bfloat16), "col").astype(jnp.float32),
    )
    sig = jax.nn.sigmoid(gate)
    silu = gate * sig
    hidden = (silu * upval).astype(jnp.bfloat16)
    contract_cols = (((1,), (1,)), ((), ()))
    grad_term = lax.dot_general(
        packed_grad, down_weight, contract_cols, preferred_element_type=jnp.float32
    )
    grad_hidden = lax.psum(grad_term.astype(jnp.bfloat16), "col").astype(jnp.float32)
    grad_gate_act = (grad_hidden * upval * sig * (1.0 + gate * (1.0 - sig))).astype(jnp.bfloat16)
    grad_up_act = (grad_hidden * silu).astype(jnp.bfloat16)
    contract_rows = (((0,), (0,)), ((), ()))
    grad_down = lax.dot_general(
        hidden, packed_grad, contract_rows, preferred_element_type=jnp.float32
    ).astype(jnp.bfloat16)
    grad_gate = lax.dot_general(
        packed, grad_gate_act, contract_rows, preferred_element_type=jnp.float32
    ).astype(jnp.bfloat16)
    grad_up = lax.dot_general(
        packed, grad_up_act, contract_rows, preferred_element_type=jnp.float32
    ).astype(jnp.bfloat16)
    term = lax.dot_general(
        grad_gate_act, gate_weight, contract_cols, preferred_element_type=jnp.float32
    )
    grad_input = sent_and_summed(
        (
            term
            + lax.dot_general(
                grad_up_act, up_weight, contract_cols, preferred_element_type=jnp.float32
            )
        ).astype(jnp.bfloat16),
        "row",
        0,
    )
    return (grad_input.astype(jnp.bfloat16), grad_gate, grad_up, grad_down)


def solution(mesh):
    return jax.shard_map(
        per_device,
        mesh=mesh,
        in_specs=(
            P(("row", "col"), None),
            P(("row", "col"), None),
            P(("row", "col")),
            P(("row", "col")),
            P(("row", "col")),
            P(("row", "col")),
            P("col", "row"),
            P("col", "row"),
            P("row", "col"),
        ),
        out_specs=(P("row", "col"), P("col", "row"), P("col", "row"), P("row", "col")),
        check_vma=False,
    )
```

profile of v0, /device:TPU:4, one launch (start us, length us, event | category | flops | bytes accessed | tf_op | source)
XLA Modules:
  0.0 991.0 jit_solution(10023484400698001869)
XLA Ops:
  7.2 0.0 copy-start
  7.2 0.0 all-gather.3.cloned.1.call-start
  9.9 0.1 maximum_bitcast_fusion
  10.0 307.3 %all-gather = f32[128,1,4]{2,1,0:T(1,128)S(1)} all-gather(f32[1,1,4]{2,1,0:T(1,128)S(1)} %maximum_bitcast_fusion), channel_id=1, replica_groups=mesh['row'=16,'col'=8] {'row','col'}, dimensions={0}, use_global_device_ids=true | all-gather | bytes 2064 | tf_op jit(solution)/shard_map/all_gather | solution.py:99
  317.3 0.1 copy.27
  317.3 0.1 convert_reduce_fusion
  317.5 0.1 select_reduce_fusion.3
  317.6 0.1 select_reduce_fusion.2
  317.7 0.1 select_reduce_fusion.1
  317.8 0.6 dynamic_slice.3
  318.4 1.8 select_convert_fusion
  320.2 0.1 copy.31
  320.3 1.1 copy.30
  321.5 0.1 pad_maximum_fusion
  321.6 0.2 copy.28
  321.8 19.5 %all_to_all.10 = bf16[84,8,512]{2,0,1:T(8,128)(2,1)S(1)} all-to-all(bf16[84,8,512]{2,0,1:T(8,128)(2,1)S(1)} %copy.28), channel_id=1, replica_groups=mesh['row'=16,'col'=8] {'col'}, dimensions={1} | all-to-all | bytes 1376256 | tf_op jit(solution)/shard_map/all_to_all | solution.py:18
  341.3 1.1 copy.29
  342.3 0.0 all-gather.3.cloned.1.call-update
  342.4 0.0 all-reduce.3.cloned.1.call-start
  342.4 0.1 reshape.149
  342.6 0.2 select_reduce_fusion
  342.8 0.1 add_select_fusion
  342.9 0.2 select_n.47
  343.0 0.1 fusion.15
  343.1 20.4 %scatter_custom_fusion = s32[2048]{0:T(1024)S(1)} fusion(s32[5376]{0:T(1024)S(1)} %fusion.15, s32[5376]{0:T(1024)S(1)} %reshape.149, s32[]{:T(128)} %constant.19.clone.1), kind=kCustom, calls=%fused_computation.47 | custom fusion | bytes 8196 | tf_op jit(solution)/shard_map/scatter | solution.py:70
  363.5 65.8 %all-gather.3.cloned.1.call-done = bf16[84,128,512]{2,1,0:T(8,128)(2,1)} async-done(((bf16[84,8,512]{2,1,0:T(8,128)(2,1)}), bf16[84,128,512]{2,1,0:T(8,128)(2,1)}) %all-gather.3.cloned.1.call-update) | async-done | bytes 11010064 | tf_op jit(solution)/shard_map/all_gather | solution.py:28
  429.3 9.6 fusion.25
  438.9 10.9 %gather_fusion = bf16[2048,512]{1,0:T(8,128)(2,1)S(1)} fusion(bf16[5376,512]{1,0:T(8,128)(2,1)} %bitcast.57, s32[2048]{0:T(1024)S(1)} %fusion.16), kind=kCustom, calls=%fused_computation.clone | custom fusion | bytes 4202496 | tf_op jit(solution)/shard_map/jit(_take)/gather | solution.py:116
  449.8 13.2 %gather_fusion.1 = bf16[2048,512]{1,0:T(8,128)(2,1)} fusion(bf16[5376,512]{1,0:T(8,128)(2,1)} %bitcast.56, s32[2048]{0:T(1024)S(1)} %fusion.16), kind=kCustom, calls=%fused_computation.1.clone | custom fusion | bytes 4202496 | tf_op jit(solution)/shard_map/jit(_take)/gather | solution.py:115
  463.0 5.9 convolution_convert_fusion
  468.9 3.9 convolution_convert_fusion.1
  472.8 3.9 convolution_convert_fusion.2
  476.6 0.0 all-reduce.3.cloned.1.call-update
  476.7 455.9 %all-reduce.3.cloned.1.call-done = (bf16[2048,924]{0,1:T(8,128)(2,1)}, bf16[2048,924]{0,1:T(8,128)(2,1)}, bf16[2048,924]{0,1:T(8,128)(2,1)}) async-done(((bf16[2048,924]{0,1:T(8,128)(2,1)}, bf16[2048,924]{0,1:T(8,128)(2,1)}, bf16[2048,924]{0,1:T(8,128)(2,1)}), (bf16[2048,924]{0,1:T(8,128)(2,1)}, bf16[2048,924]{0,1:T(8,128)(2,1)}, bf16[2048,924]{0,1:T(8,128)(2,1)})) %all-reduce.3.cloned.1.call-update) | async-done | bytes 11354128 | tf_op jit(solution)/shard_map/psum | solution.py:123
  932.6 7.3 fusion
  939.9 3.1 convolution_convert_fusion.3
  943.0 2.4 fusion.26
  945.5 3.9 add_convert_fusion
  949.4 4.5 all-to-all-start.1
  953.9 0.0 copy-start.2
  953.9 0.0 copy-start.3
  953.9 0.0 copy-start.6
  953.9 6.0 convolution_convert_fusion.4
  959.9 0.0 copy-done.3
  959.9 0.0 copy-start.1
  959.9 3.5 fusion.11
  963.4 19.8 %all-to-all-done.1 = bf16[16,128,512]{2,1,0:T(8,128)(2,1)S(1)} async-done(((bf16[16,128,512]{2,1,0:T(8,128)(2,1)}), bf16[16,128,512]{2,1,0:T(8,128)(2,1)S(1)}, u32[]{:S(2)}, u32[]{:S(2)}) %all-to-all-start.1) | async-done | bytes 2097184 | tf_op jit(solution)/shard_map/all_to_all | solution.py:40
  983.2 1.0 reduce_sum.78
  (31 shorter events, 0.2 us)
Async XLA Ops:
  7.2 455.9 %copy-start = (bf16[512,924]{0,1:T(8,128)(2,1)S(1)}, bf16[512,924]{0,1:T(8,128)(2,1)}, u32[]{:S(2)}) copy-start(bf16[512,924]{0,1:T(8,128)(2,1)} %param.17) | copy-start | bytes 2838532
  7.2 422.2 %all-gather.3.cloned.1.call-start = ((), (), s32[]{:S(2)}) async-start(), calls=%async_computation.2 | async-start | bytes 11698176 | tf_op jit(solution)/shard_map/all_gather | solution.py:28
  342.4 590.2 %all-reduce.3.cloned.1.call-start = ((), (), s32[]{:S(2)}) async-start(), calls=%async_computation.3 | async-start | bytes 22806528 | tf_op jit(solution)/shard_map/psum | solution.py:123
  449.8 23.0 %copy-start.5 = (bf16[2048,512]{1,0:T(8,128)(2,1)}, bf16[2048,512]{1,0:T(8,128)(2,1)S(1)}, u32[]{:S(2)}) copy-start(bf16[2048,512]{1,0:T(8,128)(2,1)S(1)} %gather_fusion) | copy-start | bytes 6291460
  463.0 5.9 copy-start.7
  463.0 5.9 copy-start.10
  468.9 3.9 copy-start.9
  932.6 7.3 copy-start.8
  939.9 3.2 copy-start.4
  943.0 2.4 copy-start.11
  949.4 33.8 %all-to-all-start.1 = ((bf16[16,128,512]{2,1,0:T(8,128)(2,1)}), bf16[16,128,512]{2,1,0:T(8,128)(2,1)S(1)}, u32[]{:S(2)}, u32[]{:S(2)}) async-start(bf16[16,128,512]{2,1,0:T(8,128)(2,1)} %bitcast.58), calls=%async_computation.1 | async-start | bytes 4194304 | tf_op jit(solution)/shard_map/all_to_all | solution.py:40
  953.9 6.0 copy-start.2
  953.9 6.0 copy-start.3
  953.9 6.0 copy-start.6
  959.9 24.2 %copy-start.1 = (bf16[512,924]{0,1:T(8,128)(2,1)S(1)}, bf16[512,924]{0,1:T(8,128)(2,1)}, u32[]{:S(2)}) copy-start(bf16[512,924]{0,1:T(8,128)(2,1)} %param.17) | copy-start | bytes 2838532
Sparse Core Ops, SparseCore 0:
  342.5 86.7 all-gather.2
  476.8 455.7 all-reduce.2
where the time goes:
time: 991 us
  waiting for transfers between devices  542 us (55%)
  blocking collectives  327 us (33%)
  local copies, waits for them, and re-layouts  57.6 us (6%)
  matrix products  32.5 us (3%)
  between operations  17 us (2%)
  other arithmetic  11 us (1%)
    psum x1, waiting for transfers between devices, per_device(): lax.psum(up_term.astype(jnp.bfloat16), 'col').astype(jnp.float32)  456 us
    all_gather x1, blocking collectives, per_device(): table = lax.all_gather(local, ('row', 'col'), axis=0, tiled=True)  307 us
    all_gather x1, waiting for transfers between devices, sent_together(): result = lax.all_gather(both, axis, axis=dim, tiled=True)  65.8 us
    scatter x1, local copies, waits for them, and re-layouts, source_index(): empty.at[target.reshape(-1)].set(flat_source.reshape(-1), mode='drop')  20.4 us
  transfers between devices with their start and end apart: 3, of which 3 were waited for; matrix products, arithmetic and copies ran while one was open for 3% of the time, Pallas kernels for 0%

commit v1 on v0

--- a/solution.py
+++ b/solution.py
@@ -120,7 +120,7 @@
     up_term = jnp.dot(packed, up_weight, preferred_element_type=jnp.float32)
     gate, upval = (
         lax.psum(gate_term.astype(jnp.bfloat16), "col").astype(jnp.float32),
-        lax.psum(up_term.astype(jnp.bfloat16), "col").astype(jnp.float32),
+        jnp.sum(lax.all_gather(up_term.astype(jnp.bfloat16), "col"), axis=0).astype(jnp.float32),
     )
     sig = jax.nn.sigmoid(gate)
     silu = gate * sig

time: 991 us -> 1410 us (1.42)
  waiting for transfers between devices: 542 us -> 911 us
  local copies, waits for them, and re-layouts: 57.6 us -> 84.9 us
  other arithmetic: 11 us -> 34.1 us
    all_gather x0 -> x1, waiting for transfers between devices: none -> 558 us  [per_device(): lax.all_gather(up_term.astype(jnp.bfloat16), 'col')]
    psum x1, waiting for transfers between devices: 456 us -> 267 us  [per_device(): lax.psum(grad_term.astype(jnp.bfloat16), 'col').astype(jnp.float32)]
    unnamed x26 -> x21, local copies, waits for them, and re-layouts: 1.31 us -> 29.5 us
    reduce_sum x0 -> x1, other arithmetic: none -> 23.2 us  [per_device(): jnp.sum(lax.all_gather(up_term.astype(jnp.bfloat16), 'col'), axis=0)]
  transfers between devices with their start and end apart: 3 -> 4, of which waited for: 3 -> 4; matrix products, arithmetic and copies ran while one was open for 3% -> 7% of each run, Pallas kernels for 0% -> 0%
where the time goes in v1:
time: 1410 us
  waiting for transfers between devices  911 us (65%)
  blocking collectives  327 us (23%)
  local copies, waits for them, and re-layouts  84.9 us (6%)
  other arithmetic  34.1 us (2%)
  matrix products  32.4 us (2%)
  between operations  16.7 us (1%)
    all_gather x1, waiting for transfers between devices, per_device(): lax.all_gather(up_term.astype(jnp.bfloat16), 'col')  558 us
    all_gather x1, blocking collectives, per_device(): table = lax.all_gather(local, ('row', 'col'), axis=0, tiled=True)  307 us
    psum x1, waiting for transfers between devices, per_device(): lax.psum(grad_term.astype(jnp.bfloat16), 'col').astype(jnp.float32)  267 us
    all_gather x1, waiting for transfers between devices, sent_together(): result = lax.all_gather(both, axis, axis=dim, tiled=True)  66 us
    unnamed x21, local copies, waits for them, and re-layouts  29.5 us
  transfers between devices with their start and end apart: 4, of which 4 were waited for; matrix products, arithmetic and copies ran while one was open for 7% of the time, Pallas kernels for 0%

profile of v1, /device:TPU:4, one launch (start us, length us, event | category | flops | bytes accessed | tf_op | source)
XLA Modules:
  0.0 1412.9 jit_solution(15950964044386037273)
XLA Ops:
  7.2 0.0 copy-start
  7.2 0.0 all-gather.5.cloned.1.call-start
  9.9 0.1 maximum_bitcast_fusion
  10.0 307.3 %all-gather.1 = f32[128,1,4]{2,1,0:T(1,128)S(1)} all-gather(f32[1,1,4]{2,1,0:T(1,128)S(1)} %maximum_bitcast_fusion), channel_id=1, replica_groups=mesh['row'=16,'col'=8] {'row','col'}, dimensions={0}, use_global_device_ids=true | all-gather | bytes 2064 | tf_op jit(solution)/shard_map/all_gather | solution.py:99
  317.2 0.1 copy.27
  317.3 0.1 convert_reduce_fusion
  317.5 0.1 select_reduce_fusion.3
  317.6 0.1 select_reduce_fusion.2
  317.7 0.1 select_reduce_fusion.1
  317.8 0.6 dynamic_slice.3
  318.4 1.8 select_convert_fusion
  320.2 0.1 copy.31
  320.3 1.1 copy.30
  321.5 0.1 pad_maximum_fusion
  321.6 0.2 copy.28
  321.8 19.5 %all_to_all.10 = bf16[84,8,512]{2,0,1:T(8,128)(2,1)S(1)} all-to-all(bf16[84,8,512]{2,0,1:T(8,128)(2,1)S(1)} %copy.28), channel_id=1, replica_groups=mesh['row'=16,'col'=8] {'col'}, dimensions={1} | all-to-all | bytes 1376256 | tf_op jit(solution)/shard_map/all_to_all | solution.py:18
  341.3 1.1 copy.29
  342.3 0.0 all-gather.5.cloned.1.call-update
  342.4 0.0 all-gather.7.cloned.1.call-start
  342.4 0.2 select_reduce_fusion
  342.6 0.1 add_select_fusion
  342.7 0.2 select_n.47
  342.9 0.1 reshape.149
  343.0 0.1 fusion.15
  343.1 20.2 %scatter_custom_fusion = s32[2048]{0:T(1024)S(1)} fusion(s32[5376]{0:T(1024)S(1)} %fusion.15, s32[5376]{0:T(1024)S(1)} %reshape.149, s32[]{:T(128)} %constant.44.clone.1), kind=kCustom, calls=%fused_computation.48 | custom fusion | bytes 8196 | tf_op jit(solution)/shard_map/scatter | solution.py:70
  363.3 66.0 %all-gather.5.cloned.1.call-done = bf16[84,128,512]{2,1,0:T(8,128)(2,1)} async-done(((bf16[84,8,512]{2,1,0:T(8,128)(2,1)}), bf16[84,128,512]{2,1,0:T(8,128)(2,1)}) %all-gather.5.cloned.1.call-update) | async-done | bytes 11010064 | tf_op jit(solution)/shard_map/all_gather | solution.py:28
  429.3 9.6 fusion.25
  439.0 10.9 gather_fusion.1
  449.8 5.8 convolution_convert_fusion.1
  455.7 0.0 all-gather.7.cloned.1.call-update
  455.7 0.2 all-reduce.3.cloned.1.call-start
  455.9 12.5 gather_fusion
  468.4 3.9 convolution_convert_fusion
  472.3 3.9 convolution_convert_fusion.2
  476.2 0.0 all-reduce.3.cloned.1.call-update
  476.2 558.2 %all-gather.7.cloned.1.call-done = bf16[16384,924]{0,1:T(8,128)(2,1)} async-done(((bf16[2048,924]{0,1:T(8,128)(2,1)}), bf16[16384,924]{0,1:T(8,128)(2,1)}) %all-gather.7.cloned.1.call-update) | async-done | bytes 30277648 | tf_op jit(solution)/shard_map/all_gather | solution.py:123
  1034.4 28.2 %copy.32 = bf16[116,8,8,2048]{3,2,1,0:T(8,128)(2,1)} copy(bf16[116,8,8,2048]{3,1,2,0:T(8,128)(2,1)} %bitcast.64) | data formatting | bytes 60817408
  1062.6 23.2 %bitcast_reduce_fusion = bf16[2048,924]{0,1:T(8,128)(2,1)} fusion(bf16[928,8,2048]{2,1,0:T(8,128)(2,1)} %bitcast.61), kind=kLoop, calls=%fused_computation.3 | loop fusion | flops 13246464 | bytes 34062336 | tf_op jit(solution)/shard_map/reduce_sum | solution.py:123
  1085.9 267.0 %all-reduce.3.cloned.1.call-done = (bf16[2048,924]{0,1:T(8,128)(2,1)}, bf16[2048,924]{0,1:T(8,128)(2,1)}) async-done(((bf16[2048,924]{0,1:T(8,128)(2,1)}, bf16[2048,924]{0,1:T(8,128)(2,1)}), (bf16[2048,924]{0,1:T(8,128)(2,1)}, bf16[2048,924]{0,1:T(8,128)(2,1)})) %all-reduce.3.cloned.1.call-update) | async-done | bytes 7569424 | tf_op jit(solution)/shard_map/psum | solution.py:132
  1352.9 7.1 fusion
  1360.1 3.1 convolution_convert_fusion.3
  1363.2 2.4 fusion.26
  1365.7 3.8 add_convert_fusion
  1369.4 6.7 all-to-all-start.1
  1376.1 6.0 convolution_convert_fusion.4
  1382.2 3.5 fusion.11
  1385.6 19.8 %all-to-all-done.1 = bf16[16,128,512]{2,1,0:T(8,128)(2,1)S(1)} async-done(((bf16[16,128,512]{2,1,0:T(8,128)(2,1)}), bf16[16,128,512]{2,1,0:T(8,128)(2,1)S(1)}, u32[]{:S(2)}, u32[]{:S(2)}) %all-to-all-start.1) | async-done | bytes 2097184 | tf_op jit(solution)/shard_map/all_to_all | solution.py:40
  1405.4 1.0 reduce_sum.91
  (30 shorter events, 0.2 us)
Async XLA Ops:
  7.2 461.2 %copy-start = (bf16[512,924]{0,1:T(8,128)(2,1)S(1)}, bf16[512,924]{0,1:T(8,128)(2,1)}, u32[]{:S(2)}) copy-start(bf16[512,924]{0,1:T(8,128)(2,1)} %param.17) | copy-start | bytes 2838532
  7.2 422.1 %all-gather.5.cloned.1.call-start = ((), (), s32[]{:S(2)}) async-start(), calls=%async_computation.2 | async-start | bytes 11698176 | tf_op jit(solution)/shard_map/all_gather | solution.py:28
  342.4 692.0 %all-gather.7.cloned.1.call-start = ((), (), s32[]{:S(2)}) async-start(), calls=%async_computation.3 | async-start | bytes 34209792 | tf_op jit(solution)/shard_map/all_gather | solution.py:123
  449.8 910.2 %copy-start.4 = (bf16[2048,512]{1,0:T(8,128)(2,1)}, bf16[2048,512]{1,0:T(8,128)(2,1)S(1)}, u32[]{:S(2)}) copy-start(bf16[2048,512]{1,0:T(8,128)(2,1)S(1)} %gather_fusion.1) | copy-start | bytes 6291460
  455.7 897.2 %all-reduce.3.cloned.1.call-start = ((), (), s32[]{:S(2)}) async-start(), calls=%async_computation.4 | async-start | bytes 15204352 | tf_op jit(solution)/shard_map/psum | solution.py:132
  468.4 3.9 copy-start.5
  468.4 3.9 copy-start.7
  1360.1 3.2 copy-start.3
  1363.2 2.4 copy-start.8
  1369.4 36.0 %all-to-all-start.1 = ((bf16[16,128,512]{2,1,0:T(8,128)(2,1)}), bf16[16,128,512]{2,1,0:T(8,128)(2,1)S(1)}, u32[]{:S(2)}, u32[]{:S(2)}) async-start(bf16[16,128,512]{2,1,0:T(8,128)(2,1)} %bitcast.65), calls=%async_computation.1 | async-start | bytes 4194304 | tf_op jit(solution)/shard_map/all_to_all | solution.py:40
  1376.1 6.0 copy-start.1
  1376.1 6.0 copy-start.2
  1376.1 6.0 copy-start.6
Sparse Core Ops, SparseCore 0:
  342.5 86.7 all-gather.4
  455.8 578.5 all-gather.6
  1037.0 315.8 all-reduce.2
